TPU v7x, 32 devices: a whole 2x2x4 slice. The times are simulated.
32 devices in a mesh: group: 2 (over x), frame: 16 (over z, y, core).
Axes of the slice: x: 2, y: 2, z: 4, core: 2. Of those that a mesh axis runs over, the one named last changes fastest.
Arguments:
- queries: bfloat16 [10240, 5120], P(('group', 'frame')), parts along dimension 0, may hold values from -33 to 33
- keys: bfloat16 [10240, 5120], P(('group', 'frame')), parts along dimension 0, may hold values from -33 to 33
- values: bfloat16 [10240, 5120], P(('group', 'frame')), parts along dimension 0, may hold values from -6 to 6
- labels: int32 [80], P('group'), parts along dimension 0, may hold values from 0 to 1, as said below
- band: int32 [80], P('group'), parts along dimension 0, may hold values from 2 to 4
Outputs:
- attended: bfloat16 [10240, 5120], P(('group', 'frame')), parts along dimension 0
There are 2 independent parts, one for each index of `group`. A program takes and returns all parts, laid end to end along the dimension named above; each array names one. Nothing has to cross between parts.
Inputs may be any that keep to these rules, and one draw needn't show every extreme that they name: `labels`: exactly 10 of the 40 heads carry 1, the others 0.
All inputs are finite; a program needn't handle non-finite values.
Results may differ from a plain program's by a relative error of at most 0.0049.
Values may be sent and summed in bfloat16 or wider, within the bound.
A program may use at most 128 MiB of HBM per device.

v0:
```python
import math
import jax
import jax.numpy as jnp
from jax import lax
from jax.sharding import PartitionSpec as P

TEMP_HEADS = 10


def from_partner(block, axis, bit):
    count = lax.axis_size(axis)
    route = []
    for low in range(count):
        high = low | 1 << bit
        if high != low and high < count:
            route += [(low, high), (high, low)]
    return lax.ppermute(block, axis, route)


def softmax_rounded(scores):
    peak = jnp.max(scores, axis=-1, keepdims=True)
    weights = jnp.exp(scores - peak)
    return (weights / jnp.sum(weights, axis=-1, keepdims=True)).astype(jnp.bfloat16)


def block_heads(count):
    for candidate in (6, 5, 4, 3, 2):
        if count % candidate == 0:
            return candidate
    return 1


def attend_spatial(query_part, key_all, value_all):
    head_total = query_part.shape[1]
    step_heads = block_heads(head_total)
    scale = 1.0 / math.sqrt(query_part.shape[2])

    def one_block(block_number, result):
        start = block_number * step_heads
        query_block = lax.dynamic_slice_in_dim(query_part, start, step_heads, 1)
        key_block = lax.dynamic_slice_in_dim(key_all, start, step_heads, 1)
        value_block = lax.dynamic_slice_in_dim(value_all, start, step_heads, 1)
        scores = (
            jnp.einsum("rhd,khd->hrk", query_block, key_block, preferred_element_type=jnp.float32)
            * scale
        )
        weights = softmax_rounded(scores)
        output_block = jnp.einsum(
            "hrk,khd->rhd", weights, value_block, preferred_element_type=jnp.float32
        ).astype(jnp.bfloat16)
        return lax.dynamic_update_slice_in_dim(result, output_block, start, 1)

    initial = jnp.zeros(query_part.shape, jnp.bfloat16)
    return lax.fori_loop(0, head_total // step_heads, one_block, initial)


def attend_columns(query_part, key_part, value_part, head_band):
    query_cols, key_cols, value_cols = (
        lax.all_to_all(query_part[None], "frame", split_axis=1, concat_axis=0, tiled=True),
        lax.all_to_all(key_part[None], "frame", split_axis=1, concat_axis=0, tiled=True),
        lax.all_to_all(value_part[None], "frame", split_axis=1, concat_axis=0, tiled=True),
    )
    sources, pixels, head_part, head_size = query_cols.shape
    frames = sources // 2
    scale = 1.0 / math.sqrt(head_size)
    grid_shape = (frames, 2, pixels, head_part, head_size)
    scores = (
        jnp.einsum(
            "fapnd,gapnd->apnfg",
            query_cols.reshape(grid_shape),
            key_cols.reshape(grid_shape),
            preferred_element_type=jnp.float32,
        )
        * scale
    )
    frame_ids = jnp.arange(frames, dtype=jnp.int32)
    distance = jnp.abs(frame_ids[:, None] - frame_ids[None, :])
    keep = distance[None, :, :] <= head_band[:, None, None]
    scores = jnp.where(keep, scores, jnp.float32(-1e30))
    weights = softmax_rounded(scores)
    output = jnp.einsum(
        "apnfg,gapnd->fapnd",
        weights,
        value_cols.reshape(grid_shape),
        preferred_element_type=jnp.float32,
    ).astype(jnp.bfloat16)
    output = output.reshape(sources, pixels, head_part, head_size)
    returned = lax.all_to_all(output, "frame", split_axis=0, concat_axis=1, tiled=True)
    return returned[0]


def shards(queries, keys, values, labels, band):
    row_count = queries.shape[0]
    head_count = labels.shape[0]
    head_size = queries.shape[1] // head_count
    query_heads = queries.reshape(row_count, head_count, head_size)
    key_heads = keys.reshape(row_count, head_count, head_size)
    value_heads = values.reshape(row_count, head_count, head_size)
    spatial_count = head_count - TEMP_HEADS
    ordering = jnp.argsort(labels, stable=True)
    spatial_index = ordering[:spatial_count]
    temporal_index = ordering[spatial_count:]
    inverse = jnp.argsort(ordering, stable=True)
    query_spatial = jnp.take(query_heads, spatial_index, axis=1)
    key_spatial = jnp.take(key_heads, spatial_index, axis=1)
    value_spatial = jnp.take(value_heads, spatial_index, axis=1)
    temporal_band = jnp.take(band, temporal_index)
    temporal = attend_columns(
        jnp.take(query_heads, temporal_index, axis=1),
        jnp.take(key_heads, temporal_index, axis=1),
        jnp.take(value_heads, temporal_index, axis=1),
        temporal_band,
    )
    parity = lax.axis_index("frame") % 2
    half = spatial_count // 2
    mine_start = parity * half
    other_start = (1 - parity) * half
    query_mine = lax.dynamic_slice_in_dim(query_spatial, mine_start, half, 1)
    key_mine = lax.dynamic_slice_in_dim(key_spatial, mine_start, half, 1)
    value_mine = lax.dynamic_slice_in_dim(value_spatial, mine_start, half, 1)
    query_other = lax.dynamic_slice_in_dim(query_spatial, other_start, half, 1)
    key_other = lax.dynamic_slice_in_dim(key_spatial, other_start, half, 1)
    value_other = lax.dynamic_slice_in_dim(value_spatial, other_start, half, 1)
    query_got, key_got, value_got = from_partner((query_other, key_other, value_other), "frame", 0)

    def whole_frame(own, got):
        return jnp.where(
            parity == 0, jnp.concatenate([own, got], axis=0), jnp.concatenate([got, own], axis=0)
        )

    frame_out = attend_spatial(
        whole_frame(query_mine, query_got),
        whole_frame(key_mine, key_got),
        whole_frame(value_mine, value_got),
    )
    own_rows = lax.dynamic_slice_in_dim(frame_out, parity * row_count, row_count, 0)
    other_rows = lax.dynamic_slice_in_dim(frame_out, (1 - parity) * row_count, row_count, 0)
    returned = from_partner(other_rows, "frame", 0)
    spatial = jnp.where(
        parity == 0,
        jnp.concatenate([own_rows, returned], axis=1),
        jnp.concatenate([returned, own_rows], axis=1),
    )
    combined = jnp.take(jnp.concatenate([spatial, temporal], axis=1), inverse, axis=1)
    return combined.reshape(row_count, head_count * head_size)


def solution(mesh):
    placed = (
        P(("group", "frame"), None),
        P(("group", "frame"), None),
        P(("group", "frame"), None),
        P("group"),
        P("group"),
    )
    return jax.shard_map(
        shards, mesh=mesh, in_specs=placed, out_specs=P(("group", "frame"), None), check_vma=False
    )
```

profile of v0, /device:TPU:9, one launch (start us, length us, event | category | flops | bytes accessed | tf_op | source)
XLA Modules:
  0.0 212.5 jit_solution(6797831736654225508)
XLA Ops:
  1.9 2.6 %copy_bitcast_fusion.1 = bf16[320,40,128]{2,0,1:T(8,128)(2,1)} fusion(bf16[320,5120]{1,0:T(8,128)(2,1)S(1)} %copy-done), kind=kLoop, calls=%fused_computation.30 | loop fusion | bytes 6553600 | tf_op jit(solution)/shard_map/reshape | solution.py:96
  6.7 4.7 %copy_bitcast_fusion = bf16[320,40,128]{2,0,1:T(8,128)(2,1)} fusion(bf16[320,5120]{1,0:T(8,128)(2,1)} %param.12), kind=kLoop, calls=%fused_computation.29 | loop fusion | bytes 6553600 | tf_op jit(solution)/shard_map/reshape | solution.py:97
  13.0 3.5 %gather_fusion.7 = bf16[10,320,128]{2,1,0:T(8,128)(2,1)} fusion(bf16[320,40,128]{2,0,1:T(8,128)(2,1)} %copy_bitcast_fusion, s32[1024]{0:T(1024)S(1)} %pad_clamp_fusion.1), kind=kCustom, calls=%fused_computation.5.clone | custom fusion | bytes 1638440 | tf_op jit(solution)/shard_map/jit(_take)/gather | solution.py:110
  16.5 4.5 %copy_bitcast_fusion.2 = bf16[320,40,128]{2,0,1:T(8,128)(2,1)} fusion(bf16[320,5120]{1,0:T(8,128)(2,1)} %param.13), kind=kLoop, calls=%fused_computation.31 | loop fusion | bytes 6553600 | tf_op jit(solution)/shard_map/reshape | solution.py:98
  21.0 3.5 %gather_fusion.5 = bf16[10,320,128]{2,1,0:T(8,128)(2,1)} fusion(bf16[320,40,128]{2,0,1:T(8,128)(2,1)} %copy_bitcast_fusion.2, s32[1024]{0:T(1024)S(1)} %pad_clamp_fusion.1), kind=kCustom, calls=%fused_computation.1.clone | custom fusion | bytes 1638440 | tf_op jit(solution)/shard_map/jit(_take)/gather | solution.py:111
  24.6 3.1 %select_bitcast_fusion.4 = (bf16[1,320,10,128]{3,1,2,0:T(8,128)(2,1)}, bf16[1,320,10,128]{3,1,2,0:T(8,128)(2,1)S(1)}, bf16[1,320,10,128]{3,1,2,0:T(8,128)(2,1)}) fusion(bf16[10,320,128]{2,1,0:T(8,128)(2,1)} %gather_fusion.6, pred[10]{0:T(512)(128)(4,1)S(1)} %get-tuple-element.148, bf16[10,320,128]{2,1,0:T(8,128)(2,1)} %gather_fusion.7, ...), kind=kLoop, calls=%fused_computation.50 | loop fusion | flops 1228800 | bytes 4915210 | tf_op jit(solution)/shard_map/broadcast_in_dim | solution.py:59
  29.4 6.6 %all-to-all-start.2 = ((bf16[1,320,10,128]{3,2,0,1:T(8,128)(2,1)}), bf16[1,320,10,128]{3,2,0,1:T(8,128)(2,1)}, u32[]{:S(2)}, u32[]{:S(2)}) async-start(bf16[1,320,10,128]{3,2,0,1:T(8,128)(2,1)} %copy.97), calls=%async_computation.2 | async-start | bytes 2621440 | tf_op jit(solution)/shard_map/all_to_all | solution.py:60
  36.1 4.3 %gather_fusion.4 = bf16[30,320,128]{2,1,0:T(8,128)(2,1)} fusion(bf16[320,40,128]{2,0,1:T(8,128)(2,1)} %copy_bitcast_fusion, s32[1024]{0:T(1024)S(1)} %pad_clamp_fusion.2), kind=kCustom, calls=%fused_computation.3.clone | custom fusion | bytes 4915320 | tf_op jit(solution)/shard_map/jit(_take)/gather | solution.py:105
  42.7 4.4 %gather_fusion.2 = bf16[30,320,128]{2,1,0:T(8,128)(2,1)} fusion(bf16[320,40,128]{2,0,1:T(8,128)(2,1)} %copy_bitcast_fusion.2, s32[1024]{0:T(1024)S(1)} %pad_clamp_fusion.2), kind=kCustom, calls=%fused_computation.clone | custom fusion | bytes 4915320 | tf_op jit(solution)/shard_map/jit(_take)/gather | solution.py:106
  47.1 4.6 %select_bitcast_fusion = (bf16[320,30,128]{2,0,1:T(8,128)(2,1)}, bf16[320,30,128]{2,0,1:T(8,128)(2,1)S(1)}, bf16[320,30,128]{2,0,1:T(8,128)(2,1)S(1)}) fusion(bf16[30,320,128]{2,1,0:T(8,128)(2,1)S(1)} %copy-done.5, pred[30]{0:T(512)(128)(4,1)S(1)} %get-tuple-element.146, bf16[30,320,128]{2,1,0:T(8,128)(2,1)} %gather_fusion.3, ...), kind=kLoop, calls=%fused_computation.37 | loop fusion | flops 3686400 | bytes 14745630 | tf_op jit(solution)/shard_map/jit(_take)/select_n | solution.py:105
  57.1 9.3 %all-to-all-done.2 = bf16[1,320,10,128]{3,2,0,1:T(8,128)(2,1)} async-done(((bf16[1,320,10,128]{3,2,0,1:T(8,128)(2,1)}), bf16[1,320,10,128]{3,2,0,1:T(8,128)(2,1)}, u32[]{:S(2)}, u32[]{:S(2)}) %all-to-all-start.2) | async-done | bytes 819232 | tf_op jit(solution)/shard_map/all_to_all | solution.py:60
  66.3 5.2 %all-to-all-start.1 = ((bf16[1,320,10,128]{3,2,0,1:T(8,128)(2,1)}), bf16[1,320,10,128]{3,2,0,1:T(8,128)(2,1)}, u32[]{:S(2)}, u32[]{:S(2)}) async-start(bf16[1,320,10,128]{3,2,0,1:T(8,128)(2,1)} %copy.94), calls=%async_computation.1 | async-start | bytes 2621440 | tf_op jit(solution)/shard_map/all_to_all | solution.py:59
  73.6 2.8 %copy.91 = bf16[1,320,10,128]{3,2,0,1:T(8,128)(2,1)} copy(bf16[1,320,10,128]{3,1,2,0:T(8,128)(2,1)} %get-tuple-element.163) | data formatting | bytes 1638400 | tf_op jit(solution)/shard_map/broadcast_in_dim | solution.py:61
  77.2 4.0 %maximum_select_fusion = bf16[640,15,128]{2,0,1:T(8,128)(2,1)} fusion(bf16[320,15,128]{2,0,1:T(8,128)(2,1)} %collective-permute-done, bf16[320,15,128]{2,0,1:T(8,128)(2,1)S(1)} %copy-done.8, pred[]{:T(512)S(6)} %eq.4), kind=kLoop, calls=%fused_computation.33 | loop fusion | flops 11059200 | bytes 4915201 | tf_op jit(solution)/shard_map/jit(_where)/select_n | solution.py:127
  81.2 4.0 %maximum_select_fusion.1 = bf16[640,15,128]{2,0,1:T(8,128)(2,1)} fusion(bf16[320,15,128]{2,0,1:T(8,128)(2,1)} %collective-permute-done.1, bf16[320,15,128]{2,0,1:T(8,128)(2,1)S(1)} %copy-done.9, pred[]{:T(512)S(6)} %eq.4), kind=kLoop, calls=%fused_computation.34 | loop fusion | flops 11059200 | bytes 4915201 | tf_op jit(solution)/shard_map/jit(_where)/select_n | solution.py:127
  85.2 3.8 %maximum_select_fusion.2 = bf16[640,15,128]{2,0,1:T(8,128)(2,1)} fusion(bf16[320,15,128]{2,0,1:T(8,128)(2,1)} %collective-permute-done.2, bf16[320,15,128]{2,0,1:T(8,128)(2,1)S(1)} %copy-done.10, pred[]{:T(512)S(6)} %eq.4), kind=kLoop, calls=%fused_computation.35 | loop fusion | flops 11059200 | bytes 4915201 | tf_op jit(solution)/shard_map/jit(_where)/select_n | solution.py:127
  89.0 12.9 %all-to-all-done.1 = bf16[1,320,10,128]{3,2,0,1:T(8,128)(2,1)} async-done(((bf16[1,320,10,128]{3,2,0,1:T(8,128)(2,1)}), bf16[1,320,10,128]{3,2,0,1:T(8,128)(2,1)}, u32[]{:S(2)}, u32[]{:S(2)}) %all-to-all-start.1) | async-done | bytes 819232 | tf_op jit(solution)/shard_map/all_to_all | solution.py:59
  101.9 5.3 %all-to-all-start = ((bf16[1,320,10,128]{3,2,0,1:T(8,128)(2,1)}), bf16[1,320,10,128]{3,2,0,1:T(8,128)(2,1)S(1)}, u32[]{:S(2)}, u32[]{:S(2)}) async-start(bf16[1,320,10,128]{3,2,0,1:T(8,128)(2,1)} %copy.91), calls=%async_computation | async-start | bytes 2621440 | tf_op jit(solution)/shard_map/all_to_all | solution.py:61
  109.0 50.4 %while.13 = (s32[]{:T(128)}, bf16[640,15,128]{2,0,1:T(8,128)(2,1)}, bf16[640,15,128]{2,0,1:T(8,128)(2,1)}, bf16[640,15,128]{2,0,1:T(8,128)(2,1)}, bf16[640,15,12...) while((s32[]{:T(128)}, bf16[640,15,128]{2,0,1:T(8,128)(2,1)}, ...), condition=%wide.region_5.7_spmd, body=%wide.region_2.6_spmd.sunk | while | flops 1067422080 | bytes 72116400 | solution.py:54
  109.0 2.6 %fusion.48 = f32[5,640,640]{1,2,0:T(8,128)S(1)} fusion(bf16[640,15,128]{2,0,1:T(8,128)(2,1)} %get-tuple-element.219, s32[]{:T(128)S(6)} %select_n.164, bf16[640,15,128]{2,0,1:T(8,128)(2,1)} %get-tuple-element.218), kind=kOutput, calls=%fused_computation.17.clone.1 | convolution fusion | flops 524288000 | bytes 9831424 | tf_op jit(solution)/shard_map/while/body/eval_jaxpr/rhd,khd->hrk/dot_general | solution.py:44
  114.8 8.7 %fusion.50 = bf16[640,5,128]{0,2,1:T(8,128)(2,1)S(1)} fusion(f32[5,640]{1,0:T(8,128)S(1)} %fusion.49, bf16[640,15,128]{2,0,1:T(8,128)(2,1)} %get-tuple-element.217, s32[]{:T(128)S(6)} %select_n.164, f32[5,640,640]{1,2,0:T(8,128)} %copy-done.3), kind=kOutput, calls=%fused_computation.16.clone.1 | convolution fusion | flops 534941440 | bytes 18035204 | tf_op jit(solution)/shard_map/while/body/eval_jaxpr/hrk,khd->rhd/dot_general | solution.py:48
  125.8 2.6 %fusion.48 = f32[5,640,640]{1,2,0:T(8,128)S(1)} fusion(bf16[640,15,128]{2,0,1:T(8,128)(2,1)} %get-tuple-element.219, s32[]{:T(128)S(6)} %select_n.164, bf16[640,15,128]{2,0,1:T(8,128)(2,1)} %get-tuple-element.218), kind=kOutput, calls=%fused_computation.17.clone.1 | convolution fusion | flops 524288000 | bytes 9831424 | tf_op jit(solution)/shard_map/while/body/eval_jaxpr/rhd,khd->hrk/dot_general | solution.py:44
  131.6 8.7 %fusion.50 = bf16[640,5,128]{0,2,1:T(8,128)(2,1)S(1)} fusion(f32[5,640]{1,0:T(8,128)S(1)} %fusion.49, bf16[640,15,128]{2,0,1:T(8,128)(2,1)} %get-tuple-element.217, s32[]{:T(128)S(6)} %select_n.164, f32[5,640,640]{1,2,0:T(8,128)} %copy-done.3), kind=kOutput, calls=%fused_computation.16.clone.1 | convolution fusion | flops 534941440 | bytes 18035204 | tf_op jit(solution)/shard_map/while/body/eval_jaxpr/hrk,khd->rhd/dot_general | solution.py:48
  142.6 2.6 %fusion.48 = f32[5,640,640]{1,2,0:T(8,128)S(1)} fusion(bf16[640,15,128]{2,0,1:T(8,128)(2,1)} %get-tuple-element.219, s32[]{:T(128)S(6)} %select_n.164, bf16[640,15,128]{2,0,1:T(8,128)(2,1)} %get-tuple-element.218), kind=kOutput, calls=%fused_computation.17.clone.1 | convolution fusion | flops 524288000 | bytes 9831424 | tf_op jit(solution)/shard_map/while/body/eval_jaxpr/rhd,khd->hrk/dot_general | solution.py:44
  148.4 8.7 %fusion.50 = bf16[640,5,128]{0,2,1:T(8,128)(2,1)S(1)} fusion(f32[5,640]{1,0:T(8,128)S(1)} %fusion.49, bf16[640,15,128]{2,0,1:T(8,128)(2,1)} %get-tuple-element.217, s32[]{:T(128)S(6)} %select_n.164, f32[5,640,640]{1,2,0:T(8,128)} %copy-done.3), kind=kOutput, calls=%fused_computation.16.clone.1 | convolution fusion | flops 534941440 | bytes 18035204 | tf_op jit(solution)/shard_map/while/body/eval_jaxpr/hrk,khd->rhd/dot_general | solution.py:48
  159.4 4.2 %exponential_reduce_fusion = (f32[2,20,10,8]{3,2,1,0:T(8,128)}, f32[2,20,10,8,8]{3,4,2,1,0:T(8,128)S(1)}) fusion(bf16[8,2,20,10,128]{4,3,2,1,0:T(8,128)(2,1)} %bitcast.13, bf16[8,2,20,10,128]{4,3,2,1,0:T(8,128)(2,1)} %bitcast.10, pred[10,8,8]{1,2,0:T(8,128)(4,1)S(1)} %broadcast_compare_fusion), kind=kOutput, calls=%fused_computation.43 | convolution fusion | flops 6656007 | bytes 1754240 | tf_op jit(solution)/shard_map/sub | solution.py:22
  168.0 6.0 %all-to-all-start.3 = ((bf16[16,20,10,128]{3,1,2,0:T(8,128)(2,1)}), bf16[16,20,10,128]{3,1,2,0:T(8,128)(2,1)}, u32[]{:S(2)}, u32[]{:S(2)}) async-start(bf16[16,20,10,128]{3,1,2,0:T(8,128)(2,1)} %copy.104), calls=%async_computation.3 | async-start | bytes 1966080 | tf_op jit(solution)/shard_map/all_to_all | solution.py:88
  179.9 2.7 %maximum_select_fusion.3 = bf16[320,30,128]{2,0,1:T(8,128)(2,1)S(1)} fusion(bf16[320,15,128]{2,0,1:T(8,128)(2,1)} %copy-done.12, bf16[320,15,128]{2,0,1:T(8,128)(2,1)} %get-tuple-element.150, pred[]{:T(512)S(6)} %eq.4), kind=kLoop, calls=%fused_computation.36 | loop fusion | flops 3686400 | bytes 4915201 | tf_op jit(solution)/shard_map/jit(_where)/select_n | solution.py:139
  182.6 15.1 %all-to-all-done.3 = bf16[16,20,10,128]{3,1,2,0:T(8,128)(2,1)} async-done(((bf16[16,20,10,128]{3,1,2,0:T(8,128)(2,1)}), bf16[16,20,10,128]{3,1,2,0:T(8,128)(2,1)}, u32[]{:S(2)}, u32[]{:S(2)}) %all-to-all-start.3) | async-done | bytes 819232 | tf_op jit(solution)/shard_map/all_to_all | solution.py:88
  197.7 2.4 %copy.105 = bf16[16,20,10,128]{3,1,0,2:T(8,128)(2,1)} copy(bf16[16,20,10,128]{3,1,2,0:T(8,128)(2,1)} %all-to-all-done.3) | data formatting | bytes 1638400 | tf_op jit(solution)/shard_map/all_to_all | solution.py:88
  203.3 4.9 %gather_fusion.1 = bf16[40,320,128]{2,1,0:T(8,128)(2,1)} fusion(bf16[320,40,128]{2,0,1:T(8,128)(2,1)} %pad_maximum_fusion, s32[1024]{0:T(1024)S(1)} %pad_clamp_fusion), kind=kCustom, calls=%fused_computation.7 | custom fusion | bytes 6553760 | tf_op jit(solution)/shard_map/jit(_take)/gather | solution.py:144
  208.2 4.3 %bitcast_select_fusion = bf16[320,5120]{1,0:T(8,128)(2,1)} fusion(pred[5120]{0:T(1024)(128)(4,1)S(1)} %broadcast_bitcast_fusion, bf16[40,320,128]{2,1,0:T(8,128)(2,1)} %gather_fusion.1), kind=kLoop, calls=%fused_computation.28 | loop fusion | flops 1638400 | bytes 6558720 | tf_op jit(solution)/shard_map/jit(_take)/select_n | solution.py:144
  (80 shorter events, 49.8 us)
Async XLA Ops:
  0.0 1.9 copy-start
  0.0 4.5 %copy-start.13 = (s32[40]{0:T(128)S(1)}, s32[40]{0:T(128)}, u32[]{:S(2)}) copy-start(s32[40]{0:T(128)} %param.14) | copy-start | bytes 484
  6.7 4.7 %copy-start.4 = (bf16[320,40,128]{2,0,1:T(8,128)(2,1)S(1)}, bf16[320,40,128]{2,0,1:T(8,128)(2,1)}, u32[]{:S(2)}) copy-start(bf16[320,40,128]{2,0,1:T(8,128)(2,1)} %copy_bitcast_fusion.1) | copy-start | bytes 9830404
  29.4 36.9 %all-to-all-start.2 = ((bf16[1,320,10,128]{3,2,0,1:T(8,128)(2,1)}), bf16[1,320,10,128]{3,2,0,1:T(8,128)(2,1)}, u32[]{:S(2)}, u32[]{:S(2)}) async-start(bf16[1,320,10,128]{3,2,0,1:T(8,128)(2,1)} %copy.97), calls=%async_computation.2 | async-start | bytes 2621440 | tf_op jit(solution)/shard_map/all_to_all | solution.py:60
  42.7 4.4 %copy-start.5 = (bf16[30,320,128]{2,1,0:T(8,128)(2,1)S(1)}, bf16[30,320,128]{2,1,0:T(8,128)(2,1)}, u32[]{:S(2)}) copy-start(bf16[30,320,128]{2,1,0:T(8,128)(2,1)} %gather_fusion.4) | copy-start | bytes 7372804
  53.3 23.9 %collective-permute-start = (bf16[320,15,128]{2,0,1:T(8,128)(2,1)}, bf16[320,15,128]{2,0,1:T(8,128)(2,1)}, u32[]{:S(2)}, u32[]{:S(2)}) collective-permute-start(bf16[320,15,128]{2,0,1:T(8,128)(2,1)} %get-tuple-element.157), channel_id=1, source_target_pairs={{0,1},{1,0},{2,3},{3,2},{4,5},{5,4},{6,7},{7,6},{8,9},{9,8},{10,11... | collective-permute-start | bytes 3686408 | tf_op jit(solution)/shard_map/ppermute | solution.py:17
  53.6 1.8 copy-start.11
  55.3 16.3 %copy-start.6 = (bf16[320,30,128]{2,0,1:T(8,128)(2,1)S(1)}, bf16[320,30,128]{2,0,1:T(8,128)(2,1)}, u32[]{:S(2)}) copy-start(bf16[320,30,128]{2,0,1:T(8,128)(2,1)} %get-tuple-element.158) | copy-start | bytes 7372804
  55.3 26.0 %collective-permute-start.1 = (bf16[320,15,128]{2,0,1:T(8,128)(2,1)}, bf16[320,15,128]{2,0,1:T(8,128)(2,1)}, u32[]{:S(2)}, u32[]{:S(2)}) collective-permute-start(bf16[320,15,128]{2,0,1:T(8,128)(2,1)} %get-tuple-element.155), channel_id=1, source_target_pairs={{0,1},{1,0},{2,3},{3,2},{4,5},{5,4},{6,7},{7,6},{8,9},{9,8},{10,11... | collective-permute-start | bytes 3686408 | tf_op jit(solution)/shard_map/ppermute | solution.py:17
  66.3 35.5 %all-to-all-start.1 = ((bf16[1,320,10,128]{3,2,0,1:T(8,128)(2,1)}), bf16[1,320,10,128]{3,2,0,1:T(8,128)(2,1)}, u32[]{:S(2)}, u32[]{:S(2)}) async-start(bf16[1,320,10,128]{3,2,0,1:T(8,128)(2,1)} %copy.94), calls=%async_computation.1 | async-start | bytes 2621440 | tf_op jit(solution)/shard_map/all_to_all | solution.py:59
  71.6 4.8 %copy-start.2 = (s32[40]{0:T(128)S(1)}, s32[40]{0:T(128)}, u32[]{:S(2)}) copy-start(s32[40]{0:T(128)} %param.15) | copy-start | bytes 484
  73.2 4.0 %copy-start.8 = (bf16[320,15,128]{2,0,1:T(8,128)(2,1)S(1)}, bf16[320,15,128]{2,0,1:T(8,128)(2,1)}, u32[]{:S(2)}) copy-start(bf16[320,15,128]{2,0,1:T(8,128)(2,1)} %get-tuple-element.156) | copy-start | bytes 3686404
  73.2 11.9 %collective-permute-start.2 = (bf16[320,15,128]{2,0,1:T(8,128)(2,1)}, bf16[320,15,128]{2,0,1:T(8,128)(2,1)}, u32[]{:S(2)}, u32[]{:S(2)}) collective-permute-start(bf16[320,15,128]{2,0,1:T(8,128)(2,1)} %get-tuple-element.153), channel_id=1, source_target_pairs={{0,1},{1,0},{2,3},{3,2},{4,5},{5,4},{6,7},{7,6},{8,9},{9,8},{10,11... | collective-permute-start | bytes 3686408 | tf_op jit(solution)/shard_map/ppermute | solution.py:17
  77.2 4.0 %copy-start.9 = (bf16[320,15,128]{2,0,1:T(8,128)(2,1)S(1)}, bf16[320,15,128]{2,0,1:T(8,128)(2,1)}, u32[]{:S(2)}) copy-start(bf16[320,15,128]{2,0,1:T(8,128)(2,1)} %get-tuple-element.154) | copy-start | bytes 3686404
  81.2 4.0 %copy-start.10 = (bf16[320,15,128]{2,0,1:T(8,128)(2,1)S(1)}, bf16[320,15,128]{2,0,1:T(8,128)(2,1)}, u32[]{:S(2)}) copy-start(bf16[320,15,128]{2,0,1:T(8,128)(2,1)} %get-tuple-element.152) | copy-start | bytes 3686404
  101.9 61.8 %all-to-all-start = ((bf16[1,320,10,128]{3,2,0,1:T(8,128)(2,1)}), bf16[1,320,10,128]{3,2,0,1:T(8,128)(2,1)S(1)}, u32[]{:S(2)}, u32[]{:S(2)}) async-start(bf16[1,320,10,128]{3,2,0,1:T(8,128)(2,1)} %copy.91), calls=%async_computation | async-start | bytes 2621440 | tf_op jit(solution)/shard_map/all_to_all | solution.py:61
  111.7 3.2 %copy-start.3 = (f32[5,640,640]{1,2,0:T(8,128)}, f32[5,640,640]{1,2,0:T(8,128)S(1)}, u32[]{:S(2)}) copy-start(f32[5,640,640]{1,2,0:T(8,128)S(1)} %fusion.48) | copy-start | bytes 24576004 | tf_op jit(solution)/shard_map/while
  128.4 3.2 %copy-start.3 = (f32[5,640,640]{1,2,0:T(8,128)}, f32[5,640,640]{1,2,0:T(8,128)S(1)}, u32[]{:S(2)}) copy-start(f32[5,640,640]{1,2,0:T(8,128)S(1)} %fusion.48) | copy-start | bytes 24576004 | tf_op jit(solution)/shard_map/while
  145.2 3.2 %copy-start.3 = (f32[5,640,640]{1,2,0:T(8,128)}, f32[5,640,640]{1,2,0:T(8,128)S(1)}, u32[]{:S(2)}) copy-start(f32[5,640,640]{1,2,0:T(8,128)S(1)} %fusion.48) | copy-start | bytes 24576004 | tf_op jit(solution)/shard_map/while
  165.5 8.6 %copy-start.7 = (bf16[640,15,128]{2,0,1:T(8,128)(2,1)S(1)}, bf16[640,15,128]{2,0,1:T(8,128)(2,1)}, u32[]{:S(2)}) copy-start(bf16[640,15,128]{2,0,1:T(8,128)(2,1)} %get-tuple-element.105) | copy-start | bytes 7372804
  168.0 29.6 %all-to-all-start.3 = ((bf16[16,20,10,128]{3,1,2,0:T(8,128)(2,1)}), bf16[16,20,10,128]{3,1,2,0:T(8,128)(2,1)}, u32[]{:S(2)}, u32[]{:S(2)}) async-start(bf16[16,20,10,128]{3,1,2,0:T(8,128)(2,1)} %copy.104), calls=%async_computation.3 | async-start | bytes 1966080 | tf_op jit(solution)/shard_map/all_to_all | solution.py:88
  175.7 3.1 %collective-permute-start.3 = (bf16[320,15,128]{2,0,1:T(8,128)(2,1)}, bf16[320,15,128]{2,0,1:T(8,128)(2,1)S(1)}, u32[]{:S(2)}, u32[]{:S(2)}) collective-permute-start(bf16[320,15,128]{2,0,1:T(8,128)(2,1)} %get-tuple-element.151), channel_id=1, source_target_pairs={{0,1},{1,0},{2,3},{3,2},{4,5},{5,4},{6,7},{7,6},{8,9},{9,8},{10,11... | collective-permute-start | bytes 3686408 | tf_op jit(solution)/shard_map/ppermute | solution.py:17
  178.8 1.0 copy-start.12
  203.3 9.2 %copy-start.1 = (bf16[320,5120]{1,0:T(8,128)(2,1)S(1)}, bf16[320,5120]{1,0:T(8,128)(2,1)}, u32[]{:S(2)}) copy-start(bf16[320,5120]{1,0:T(8,128)(2,1)} %param.11) | copy-start | bytes 9830404
where the time goes:
time: 213 us
  local copies, waits for them, and re-layouts  71.1 us (33%)
  matrix products  39.9 us (19%)
  other arithmetic  39.1 us (18%)
  waiting for transfers between devices  37.8 us (18%)
  starting transfers between devices  24.4 us (11%)
    dot_general x3, matrix products, one_block(): jnp.einsum('hrk,khd->rhd', weights, value_block, preferred_element_type=j...  26 us
    all_to_all x1, waiting for transfers between devices, attend_columns(): lax.all_to_all(output, 'frame', split_axis=0, concat_axis=1, tiled=True)  15.1 us
    all_to_all x1, waiting for transfers between devices, attend_columns(): lax.all_to_all(query_part[None], 'frame', split_axis=1, concat_axis=0, ti...  12.9 us
    select_n x3, other arithmetic, whole_frame(): jnp.where(parity == 0, jnp.concatenate([own, got], axis=0), jnp.concatena...  11.7 us
    all_to_all x1, waiting for transfers between devices, attend_columns(): lax.all_to_all(key_part[None], 'frame', split_axis=1, concat_axis=0, tile...  9.25 us
    dot_general x3, matrix products, one_block(): jnp.einsum('rhd,khd->hrk', query_block, key_block, preferred_element_type...  7.85 us
    dynamic_update_slice x6, local copies, waits for them, and re-layouts, one_block(): return lax.dynamic_update_slice_in_dim(result, output_block, start, 1)  7.02 us
    all_to_all x1, starting transfers between devices, attend_columns(): lax.all_to_all(key_part[None], 'frame', split_axis=1, concat_axis=0, tile...  6.61 us
  transfers between devices with their start and end apart: 8, of which 4 were waited for; matrix products, arithmetic and copies ran while one was open for 46% of the time, Pallas kernels for 0%

commit v1 on v0

--- a/solution.py
+++ b/solution.py
@@ -5,6 +5,13 @@
 from jax.sharding import PartitionSpec as P
 
 TEMP_HEADS = 10
+
+
+def take_slices(content, on_dim, array_dim):
+    seen_now = lax.axis_size("frame")
+    local_out = jnp.split(content, seen_now, on_dim)
+    tmp = jnp.stack(local_out, 0)
+    return jnp.concatenate(lax.all_to_all(tmp, "frame", 0, 0), array_dim)
 
 
 def from_partner(block, axis, bit):
@@ -56,7 +63,7 @@
 
 def attend_columns(query_part, key_part, value_part, head_band):
     query_cols, key_cols, value_cols = (
-        lax.all_to_all(query_part[None], "frame", split_axis=1, concat_axis=0, tiled=True),
+        take_slices(query_part[None], 1, 0),
         lax.all_to_all(key_part[None], "frame", split_axis=1, concat_axis=0, tiled=True),
         lax.all_to_all(value_part[None], "frame", split_axis=1, concat_axis=0, tiled=True),
     )

time: 213 us -> 203 us (0.953)
  waiting for transfers between devices: 37.8 us -> 22.6 us
  local copies, waits for them, and re-layouts: 71.1 us -> 75.7 us
    all_to_all x1, waiting for transfers between devices: 9.25 us -> 0.71 us  [attend_columns(): lax.all_to_all(key_part[None], 'frame', split_axis=1, concat_axis=0, tile...]
    unnamed x26 -> x41, local copies, waits for them, and re-layouts: 3.02 us -> 10.7 us
    all_to_all x1, waiting for transfers between devices: 12.9 us -> 6.21 us  [take_slices(): return jnp.concatenate(lax.all_to_all(tmp, 'frame', 0, 0), array_dim)]
  transfers between devices with their start and end apart: 8 -> 8, of which waited for: 4 -> 4; matrix products, arithmetic and copies ran while one was open for 46% -> 52% of each run, Pallas kernels for 0% -> 0%
where the time goes in v1:
time: 203 us; the launch traced here: 202 us
  local copies, waits for them, and re-layouts  75.7 us (37%)
  other arithmetic  39.9 us (20%)
  matrix products  39.7 us (20%)
  starting transfers between devices  24.1 us (12%)
  waiting for transfers between devices  22.6 us (11%)
    dot_general x3, matrix products, one_block(): jnp.einsum('hrk,khd->rhd', weights, value_block, preferred_element_type=j...  26 us
    all_to_all x1, waiting for transfers between devices, attend_columns(): lax.all_to_all(output, 'frame', split_axis=0, concat_axis=1, tiled=True)  15.1 us
    select_n x3, other arithmetic, whole_frame(): jnp.where(parity == 0, jnp.concatenate([own, got], axis=0), jnp.concatena...  11.7 us
    unnamed x41, local copies, waits for them, and re-layouts  10.7 us
    dot_general x3, matrix products, one_block(): jnp.einsum('rhd,khd->hrk', query_block, key_block, preferred_element_type...  7.85 us
    dynamic_update_slice x6, local copies, waits for them, and re-layouts, one_block(): return lax.dynamic_update_slice_in_dim(result, output_block, start, 1)  7.02 us
    all_to_all x1, starting transfers between devices, attend_columns(): lax.all_to_all(key_part[None], 'frame', split_axis=1, concat_axis=0, tile...  6.61 us
    sub x3, other arithmetic, softmax_rounded(): weights = jnp.exp(scores - peak)  6.35 us
  transfers between devices with their start and end apart: 8, of which 4 were waited for; matrix products, arithmetic and copies ran while one was open for 52% of the time, Pallas kernels for 0%

profile of v1, /device:TPU:9, one launch (start us, length us, event | category | flops | bytes accessed | tf_op | source)
XLA Modules:
  0.0 202.3 jit_solution(3691809183805339185)
XLA Ops:
  0.0 2.8 %sort.31 = (s32[40]{0:T(128)}, s32[40]{0:T(128)S(1)}) sort(s32[40]{0:T(128)} %param.14, s32[40]{0:T(128)S(1)} %iota.21), dimensions={0}, to_apply=%region_0.0 | sort | flops 240 | bytes 640 | tf_op jit(solution)/shard_map/jit(argsort)/sort | solution.py:107
  3.0 2.6 %copy_bitcast_fusion.1 = bf16[320,40,128]{2,0,1:T(8,128)(2,1)} fusion(bf16[320,5120]{1,0:T(8,128)(2,1)S(1)} %copy-done), kind=kLoop, calls=%fused_computation.30 | loop fusion | bytes 6553600 | tf_op jit(solution)/shard_map/reshape | solution.py:103
  5.6 2.6 %copy_bitcast_fusion = bf16[320,40,128]{2,0,1:T(8,128)(2,1)} fusion(bf16[320,5120]{1,0:T(8,128)(2,1)S(1)} %copy-done.12), kind=kLoop, calls=%fused_computation.29 | loop fusion | bytes 6553600 | tf_op jit(solution)/shard_map/reshape | solution.py:104
  9.8 3.5 %gather_fusion.7 = bf16[10,320,128]{2,1,0:T(8,128)(2,1)} fusion(bf16[320,40,128]{2,0,1:T(8,128)(2,1)} %copy_bitcast_fusion, s32[1024]{0:T(1024)S(1)} %get-tuple-element.166), kind=kCustom, calls=%fused_computation.5.clone | custom fusion | bytes 1638440 | tf_op jit(solution)/shard_map/jit(_take)/gather | solution.py:117
  13.3 4.5 %copy_bitcast_fusion.2 = bf16[320,40,128]{2,0,1:T(8,128)(2,1)} fusion(bf16[320,5120]{1,0:T(8,128)(2,1)} %param.13), kind=kLoop, calls=%fused_computation.31 | loop fusion | bytes 6553600 | tf_op jit(solution)/shard_map/reshape | solution.py:105
  17.9 3.5 %gather_fusion.5 = bf16[10,320,128]{2,1,0:T(8,128)(2,1)} fusion(bf16[320,40,128]{2,0,1:T(8,128)(2,1)} %copy_bitcast_fusion.2, s32[1024]{0:T(1024)S(1)} %get-tuple-element.166), kind=kCustom, calls=%fused_computation.1.clone | custom fusion | bytes 1638440 | tf_op jit(solution)/shard_map/jit(_take)/gather | solution.py:118
  21.4 3.1 %select_bitcast_fusion.4 = (bf16[1,320,10,128]{3,1,2,0:T(8,128)(2,1)}, bf16[1,320,10,128]{3,1,2,0:T(8,128)(2,1)S(1)}, bf16[1,320,10,128]{3,1,2,0:T(8,128)(2,1)}) fusion(bf16[10,320,128]{2,1,0:T(8,128)(2,1)} %gather_fusion.6, pred[10]{0:T(512)(128)(4,1)S(1)} %get-tuple-element.148, bf16[10,320,128]{2,1,0:T(8,128)(2,1)} %gather_fusion.7, ...), kind=kLoop, calls=%fused_computation.50 | loop fusion | flops 1228800 | bytes 4915210 | tf_op jit(solution)/shard_map/broadcast_in_dim | solution.py:66
  26.3 6.6 %all-to-all-start.2 = ((bf16[1,320,10,128]{3,2,0,1:T(8,128)(2,1)}), bf16[1,320,10,128]{3,2,0,1:T(8,128)(2,1)}, u32[]{:S(2)}, u32[]{:S(2)}) async-start(bf16[1,320,10,128]{3,2,0,1:T(8,128)(2,1)} %copy.96), calls=%async_computation.2 | async-start | bytes 2621440 | tf_op jit(solution)/shard_map/all_to_all | solution.py:67
  32.9 4.3 %gather_fusion.4 = bf16[30,320,128]{2,1,0:T(8,128)(2,1)} fusion(bf16[320,40,128]{2,0,1:T(8,128)(2,1)} %copy_bitcast_fusion, s32[1024]{0:T(1024)S(1)} %get-tuple-element.167), kind=kCustom, calls=%fused_computation.3.clone | custom fusion | bytes 4915320 | tf_op jit(solution)/shard_map/jit(_take)/gather | solution.py:112
  39.5 4.4 %gather_fusion.2 = bf16[30,320,128]{2,1,0:T(8,128)(2,1)} fusion(bf16[320,40,128]{2,0,1:T(8,128)(2,1)} %copy_bitcast_fusion.2, s32[1024]{0:T(1024)S(1)} %get-tuple-element.167), kind=kCustom, calls=%fused_computation.clone | custom fusion | bytes 4915320 | tf_op jit(solution)/shard_map/jit(_take)/gather | solution.py:113
  43.9 4.6 %select_bitcast_fusion = (bf16[320,30,128]{2,0,1:T(8,128)(2,1)}, bf16[320,30,128]{2,0,1:T(8,128)(2,1)S(1)}, bf16[320,30,128]{2,0,1:T(8,128)(2,1)S(1)}) fusion(bf16[30,320,128]{2,1,0:T(8,128)(2,1)S(1)} %copy-done.5, pred[30]{0:T(512)(128)(4,1)S(1)} %get-tuple-element.146, bf16[30,320,128]{2,1,0:T(8,128)(2,1)} %gather_fusion.3, ...), kind=kLoop, calls=%fused_computation.37 | loop fusion | flops 3686400 | bytes 14745630 | tf_op jit(solution)/shard_map/jit(_take)/select_n | solution.py:112
  63.2 5.3 %all-to-all-start.1 = ((bf16[16,1,20,10,128]{4,2,3,1,0:T(8,128)(2,1)}), bf16[16,1,20,10,128]{4,2,3,1,0:T(8,128)(2,1)}, u32[]{:S(2)}, u32[]{:S(2)}) async-start(bf16[16,1,20,10,128]{4,2,3,1,0:T(8,128)(2,1)} %fusion.28), calls=%async_computation.1 | async-start | bytes 1966080 | tf_op jit(solution)/shard_map/all_to_all | solution.py:14
  70.5 2.8 %copy.91 = bf16[1,320,10,128]{3,2,0,1:T(8,128)(2,1)} copy(bf16[1,320,10,128]{3,1,2,0:T(8,128)(2,1)} %get-tuple-element.163) | data formatting | bytes 1638400 | tf_op jit(solution)/shard_map/broadcast_in_dim | solution.py:68
  74.1 4.0 %maximum_select_fusion = bf16[640,15,128]{2,0,1:T(8,128)(2,1)} fusion(bf16[320,15,128]{2,0,1:T(8,128)(2,1)} %collective-permute-done, bf16[320,15,128]{2,0,1:T(8,128)(2,1)S(1)} %copy-done.8, pred[]{:T(512)S(6)} %eq.4), kind=kLoop, calls=%fused_computation.33 | loop fusion | flops 11059200 | bytes 4915201 | tf_op jit(solution)/shard_map/jit(_where)/select_n | solution.py:134
  78.1 3.9 %maximum_select_fusion.1 = bf16[640,15,128]{2,0,1:T(8,128)(2,1)} fusion(bf16[320,15,128]{2,0,1:T(8,128)(2,1)} %collective-permute-done.1, bf16[320,15,128]{2,0,1:T(8,128)(2,1)S(1)} %copy-done.9, pred[]{:T(512)S(6)} %eq.4), kind=kLoop, calls=%fused_computation.34 | loop fusion | flops 11059200 | bytes 4915201 | tf_op jit(solution)/shard_map/jit(_where)/select_n | solution.py:134
  82.1 3.8 %maximum_select_fusion.2 = bf16[640,15,128]{2,0,1:T(8,128)(2,1)} fusion(bf16[320,15,128]{2,0,1:T(8,128)(2,1)} %collective-permute-done.2, bf16[320,15,128]{2,0,1:T(8,128)(2,1)S(1)} %copy-done.10, pred[]{:T(512)S(6)} %eq.4), kind=kLoop, calls=%fused_computation.35 | loop fusion | flops 11059200 | bytes 4915201 | tf_op jit(solution)/shard_map/jit(_where)/select_n | solution.py:134
  85.9 6.2 %all-to-all-done.1 = bf16[16,1,20,10,128]{4,2,3,1,0:T(8,128)(2,1)} async-done(((bf16[16,1,20,10,128]{4,2,3,1,0:T(8,128)(2,1)}), bf16[16,1,20,10,128]{4,2,3,1,0:T(8,128)(2,1)}, u32[]{:S(2)}, u32[]{:S(2)}) %all-to-all-start.1) | async-done | bytes 819232 | tf_op jit(solution)/shard_map/all_to_all | solution.py:14
  92.1 4.9 %all-to-all-start = ((bf16[1,320,10,128]{3,2,0,1:T(8,128)(2,1)}), bf16[1,320,10,128]{3,2,0,1:T(8,128)(2,1)S(1)}, u32[]{:S(2)}, u32[]{:S(2)}) async-start(bf16[1,320,10,128]{3,2,0,1:T(8,128)(2,1)} %copy.91), calls=%async_computation | async-start | bytes 2621440 | tf_op jit(solution)/shard_map/all_to_all | solution.py:68
  98.9 50.3 %while.13 = (s32[]{:T(128)}, bf16[640,15,128]{2,0,1:T(8,128)(2,1)}, bf16[640,15,128]{2,0,1:T(8,128)(2,1)}, bf16[640,15,128]{2,0,1:T(8,128)(2,1)}, bf16[640,15,12...) while((s32[]{:T(128)}, bf16[640,15,128]{2,0,1:T(8,128)(2,1)}, ...), condition=%wide.region_5.7_spmd, body=%wide.region_2.6_spmd.sunk | while | flops 1067422080 | bytes 72116400 | solution.py:61
  98.9 2.6 %fusion.64 = f32[5,640,640]{1,2,0:T(8,128)S(1)} fusion(bf16[640,15,128]{2,0,1:T(8,128)(2,1)} %get-tuple-element.221, s32[]{:T(128)S(6)} %select_n.164, bf16[640,15,128]{2,0,1:T(8,128)(2,1)} %get-tuple-element.220), kind=kOutput, calls=%fused_computation.17.clone.1 | convolution fusion | flops 524288000 | bytes 9831424 | tf_op jit(solution)/shard_map/while/body/eval_jaxpr/rhd,khd->hrk/dot_general | solution.py:51
  104.7 8.7 %fusion.66 = bf16[640,5,128]{0,2,1:T(8,128)(2,1)S(1)} fusion(f32[5,640]{1,0:T(8,128)S(1)} %fusion.65, bf16[640,15,128]{2,0,1:T(8,128)(2,1)} %get-tuple-element.219, s32[]{:T(128)S(6)} %select_n.164, f32[5,640,640]{1,2,0:T(8,128)} %copy-done.3), kind=kOutput, calls=%fused_computation.16.clone.1 | convolution fusion | flops 534941440 | bytes 18035204 | tf_op jit(solution)/shard_map/while/body/eval_jaxpr/hrk,khd->rhd/dot_general | solution.py:55
  115.7 2.6 %fusion.64 = f32[5,640,640]{1,2,0:T(8,128)S(1)} fusion(bf16[640,15,128]{2,0,1:T(8,128)(2,1)} %get-tuple-element.221, s32[]{:T(128)S(6)} %select_n.164, bf16[640,15,128]{2,0,1:T(8,128)(2,1)} %get-tuple-element.220), kind=kOutput, calls=%fused_computation.17.clone.1 | convolution fusion | flops 524288000 | bytes 9831424 | tf_op jit(solution)/shard_map/while/body/eval_jaxpr/rhd,khd->hrk/dot_general | solution.py:51
  121.5 8.7 %fusion.66 = bf16[640,5,128]{0,2,1:T(8,128)(2,1)S(1)} fusion(f32[5,640]{1,0:T(8,128)S(1)} %fusion.65, bf16[640,15,128]{2,0,1:T(8,128)(2,1)} %get-tuple-element.219, s32[]{:T(128)S(6)} %select_n.164, f32[5,640,640]{1,2,0:T(8,128)} %copy-done.3), kind=kOutput, calls=%fused_computation.16.clone.1 | convolution fusion | flops 534941440 | bytes 18035204 | tf_op jit(solution)/shard_map/while/body/eval_jaxpr/hrk,khd->rhd/dot_general | solution.py:55
  132.5 2.6 %fusion.64 = f32[5,640,640]{1,2,0:T(8,128)S(1)} fusion(bf16[640,15,128]{2,0,1:T(8,128)(2,1)} %get-tuple-element.221, s32[]{:T(128)S(6)} %select_n.164, bf16[640,15,128]{2,0,1:T(8,128)(2,1)} %get-tuple-element.220), kind=kOutput, calls=%fused_computation.17.clone.1 | convolution fusion | flops 524288000 | bytes 9831424 | tf_op jit(solution)/shard_map/while/body/eval_jaxpr/rhd,khd->hrk/dot_general | solution.py:51
  138.2 8.7 %fusion.66 = bf16[640,5,128]{0,2,1:T(8,128)(2,1)S(1)} fusion(f32[5,640]{1,0:T(8,128)S(1)} %fusion.65, bf16[640,15,128]{2,0,1:T(8,128)(2,1)} %get-tuple-element.219, s32[]{:T(128)S(6)} %select_n.164, f32[5,640,640]{1,2,0:T(8,128)} %copy-done.3), kind=kOutput, calls=%fused_computation.16.clone.1 | convolution fusion | flops 534941440 | bytes 18035204 | tf_op jit(solution)/shard_map/while/body/eval_jaxpr/hrk,khd->rhd/dot_general | solution.py:55
  149.3 4.1 %exponential_reduce_fusion = (f32[2,20,10,8]{3,2,1,0:T(8,128)}, f32[2,20,10,8,8]{3,4,2,1,0:T(8,128)S(1)}) fusion(bf16[8,2,20,10,128]{4,3,2,1,0:T(8,128)(2,1)} %bitcast.30, bf16[8,2,20,10,128]{4,2,3,1,0:T(8,128)(2,1)} %bitcast.27, pred[10,8,8]{1,2,0:T(8,128)(4,1)S(1)} %broadcast_compare_fusion), kind=kOutput, calls=%fused_computation.43 | convolution fusion | flops 6656007 | bytes 1754240 | tf_op jit(solution)/shard_map/sub | solution.py:29
  157.7 6.0 %all-to-all-start.3 = ((bf16[16,20,10,128]{3,1,2,0:T(8,128)(2,1)}), bf16[16,20,10,128]{3,1,2,0:T(8,128)(2,1)}, u32[]{:S(2)}, u32[]{:S(2)}) async-start(bf16[16,20,10,128]{3,1,2,0:T(8,128)(2,1)} %copy.103), calls=%async_computation.3 | async-start | bytes 1966080 | tf_op jit(solution)/shard_map/all_to_all | solution.py:95
  169.6 2.6 %maximum_select_fusion.3 = bf16[320,30,128]{2,0,1:T(8,128)(2,1)S(1)} fusion(bf16[320,15,128]{2,0,1:T(8,128)(2,1)} %copy-done.13, bf16[320,15,128]{2,0,1:T(8,128)(2,1)} %get-tuple-element.150, pred[]{:T(512)S(6)} %eq.4), kind=kLoop, calls=%fused_computation.36 | loop fusion | flops 3686400 | bytes 4915201 | tf_op jit(solution)/shard_map/jit(_where)/select_n | solution.py:146
  172.2 15.1 %all-to-all-done.3 = bf16[16,20,10,128]{3,1,2,0:T(8,128)(2,1)} async-done(((bf16[16,20,10,128]{3,1,2,0:T(8,128)(2,1)}), bf16[16,20,10,128]{3,1,2,0:T(8,128)(2,1)}, u32[]{:S(2)}, u32[]{:S(2)}) %all-to-all-start.3) | async-done | bytes 819232 | tf_op jit(solution)/shard_map/all_to_all | solution.py:95
  187.4 2.4 %copy.104 = bf16[16,20,10,128]{3,1,0,2:T(8,128)(2,1)} copy(bf16[16,20,10,128]{3,1,2,0:T(8,128)(2,1)} %all-to-all-done.3) | data formatting | bytes 1638400 | tf_op jit(solution)/shard_map/all_to_all | solution.py:95
  193.0 4.9 %gather_fusion.1 = bf16[40,320,128]{2,1,0:T(8,128)(2,1)} fusion(bf16[320,40,128]{2,0,1:T(8,128)(2,1)} %pad_maximum_fusion, s32[1024]{0:T(1024)S(1)} %pad_clamp_fusion), kind=kCustom, calls=%fused_computation.7 | custom fusion | bytes 6553760 | tf_op jit(solution)/shard_map/jit(_take)/gather | solution.py:151
  197.9 4.3 %bitcast_select_fusion = bf16[320,5120]{1,0:T(8,128)(2,1)} fusion(pred[5120]{0:T(1024)(128)(4,1)S(1)} %broadcast_bitcast_fusion, bf16[40,320,128]{2,1,0:T(8,128)(2,1)} %gather_fusion.1), kind=kLoop, calls=%fused_computation.28 | loop fusion | flops 1638400 | bytes 6558720 | tf_op jit(solution)/shard_map/jit(_take)/select_n | solution.py:151
  (94 shorter events, 55.1 us)
Async XLA Ops:
  0.0 2.9 %copy-start = (bf16[320,5120]{1,0:T(8,128)(2,1)S(1)}, bf16[320,5120]{1,0:T(8,128)(2,1)}, u32[]{:S(2)}) copy-start(bf16[320,5120]{1,0:T(8,128)(2,1)} %param.11) | copy-start | bytes 9830404
  2.9 2.6 %copy-start.12 = (bf16[320,5120]{1,0:T(8,128)(2,1)S(1)}, bf16[320,5120]{1,0:T(8,128)(2,1)}, u32[]{:S(2)}) copy-start(bf16[320,5120]{1,0:T(8,128)(2,1)} %param.12) | copy-start | bytes 9830404
  5.6 2.6 %copy-start.4 = (bf16[320,40,128]{2,0,1:T(8,128)(2,1)S(1)}, bf16[320,40,128]{2,0,1:T(8,128)(2,1)}, u32[]{:S(2)}) copy-start(bf16[320,40,128]{2,0,1:T(8,128)(2,1)} %copy_bitcast_fusion.1) | copy-start | bytes 9830404
  26.3 36.9 %all-to-all-start.2 = ((bf16[1,320,10,128]{3,2,0,1:T(8,128)(2,1)}), bf16[1,320,10,128]{3,2,0,1:T(8,128)(2,1)}, u32[]{:S(2)}, u32[]{:S(2)}) async-start(bf16[1,320,10,128]{3,2,0,1:T(8,128)(2,1)} %copy.96), calls=%async_computation.2 | async-start | bytes 2621440 | tf_op jit(solution)/shard_map/all_to_all | solution.py:67
  39.5 4.4 %copy-start.5 = (bf16[30,320,128]{2,1,0:T(8,128)(2,1)S(1)}, bf16[30,320,128]{2,1,0:T(8,128)(2,1)}, u32[]{:S(2)}) copy-start(bf16[30,320,128]{2,1,0:T(8,128)(2,1)} %gather_fusion.4) | copy-start | bytes 7372804
  50.1 24.0 %collective-permute-start = (bf16[320,15,128]{2,0,1:T(8,128)(2,1)}, bf16[320,15,128]{2,0,1:T(8,128)(2,1)}, u32[]{:S(2)}, u32[]{:S(2)}) collective-permute-start(bf16[320,15,128]{2,0,1:T(8,128)(2,1)} %get-tuple-element.157), channel_id=1, source_target_pairs={{0,1},{1,0},{2,3},{3,2},{4,5},{5,4},{6,7},{7,6},{8,9},{9,8},{10,11... | collective-permute-start | bytes 3686408 | tf_op jit(solution)/shard_map/ppermute | solution.py:24
  50.5 1.8 copy-start.11
  52.1 16.4 %copy-start.6 = (bf16[320,30,128]{2,0,1:T(8,128)(2,1)S(1)}, bf16[320,30,128]{2,0,1:T(8,128)(2,1)}, u32[]{:S(2)}) copy-start(bf16[320,30,128]{2,0,1:T(8,128)(2,1)} %get-tuple-element.158) | copy-start | bytes 7372804
  52.1 26.0 %collective-permute-start.1 = (bf16[320,15,128]{2,0,1:T(8,128)(2,1)}, bf16[320,15,128]{2,0,1:T(8,128)(2,1)}, u32[]{:S(2)}, u32[]{:S(2)}) collective-permute-start(bf16[320,15,128]{2,0,1:T(8,128)(2,1)} %get-tuple-element.155), channel_id=1, source_target_pairs={{0,1},{1,0},{2,3},{3,2},{4,5},{5,4},{6,7},{7,6},{8,9},{9,8},{10,11... | collective-permute-start | bytes 3686408 | tf_op jit(solution)/shard_map/ppermute | solution.py:24
  63.2 28.9 %all-to-all-start.1 = ((bf16[16,1,20,10,128]{4,2,3,1,0:T(8,128)(2,1)}), bf16[16,1,20,10,128]{4,2,3,1,0:T(8,128)(2,1)}, u32[]{:S(2)}, u32[]{:S(2)}) async-start(bf16[16,1,20,10,128]{4,2,3,1,0:T(8,128)(2,1)} %fusion.28), calls=%async_computation.1 | async-start | bytes 1966080 | tf_op jit(solution)/shard_map/all_to_all | solution.py:14
  68.5 4.9 %copy-start.2 = (s32[40]{0:T(128)S(1)}, s32[40]{0:T(128)}, u32[]{:S(2)}) copy-start(s32[40]{0:T(128)} %param.15) | copy-start | bytes 484
  70.1 4.0 %copy-start.8 = (bf16[320,15,128]{2,0,1:T(8,128)(2,1)S(1)}, bf16[320,15,128]{2,0,1:T(8,128)(2,1)}, u32[]{:S(2)}) copy-start(bf16[320,15,128]{2,0,1:T(8,128)(2,1)} %get-tuple-element.156) | copy-start | bytes 3686404
  70.1 12.0 %collective-permute-start.2 = (bf16[320,15,128]{2,0,1:T(8,128)(2,1)}, bf16[320,15,128]{2,0,1:T(8,128)(2,1)}, u32[]{:S(2)}, u32[]{:S(2)}) collective-permute-start(bf16[320,15,128]{2,0,1:T(8,128)(2,1)} %get-tuple-element.153), channel_id=1, source_target_pairs={{0,1},{1,0},{2,3},{3,2},{4,5},{5,4},{6,7},{7,6},{8,9},{9,8},{10,11... | collective-permute-start | bytes 3686408 | tf_op jit(solution)/shard_map/ppermute | solution.py:24
  74.1 4.0 %copy-start.9 = (bf16[320,15,128]{2,0,1:T(8,128)(2,1)S(1)}, bf16[320,15,128]{2,0,1:T(8,128)(2,1)}, u32[]{:S(2)}) copy-start(bf16[320,15,128]{2,0,1:T(8,128)(2,1)} %get-tuple-element.154) | copy-start | bytes 3686404
  78.1 4.0 %copy-start.10 = (bf16[320,15,128]{2,0,1:T(8,128)(2,1)S(1)}, bf16[320,15,128]{2,0,1:T(8,128)(2,1)}, u32[]{:S(2)}) copy-start(bf16[320,15,128]{2,0,1:T(8,128)(2,1)} %get-tuple-element.152) | copy-start | bytes 3686404
  92.1 61.3 %all-to-all-start = ((bf16[1,320,10,128]{3,2,0,1:T(8,128)(2,1)}), bf16[1,320,10,128]{3,2,0,1:T(8,128)(2,1)S(1)}, u32[]{:S(2)}, u32[]{:S(2)}) async-start(bf16[1,320,10,128]{3,2,0,1:T(8,128)(2,1)} %copy.91), calls=%async_computation | async-start | bytes 2621440 | tf_op jit(solution)/shard_map/all_to_all | solution.py:68
  101.5 3.2 %copy-start.3 = (f32[5,640,640]{1,2,0:T(8,128)}, f32[5,640,640]{1,2,0:T(8,128)S(1)}, u32[]{:S(2)}) copy-start(f32[5,640,640]{1,2,0:T(8,128)S(1)} %fusion.64) | copy-start | bytes 24576004 | tf_op jit(solution)/shard_map/while
  118.3 3.2 %copy-start.3 = (f32[5,640,640]{1,2,0:T(8,128)}, f32[5,640,640]{1,2,0:T(8,128)S(1)}, u32[]{:S(2)}) copy-start(f32[5,640,640]{1,2,0:T(8,128)S(1)} %fusion.64) | copy-start | bytes 24576004 | tf_op jit(solution)/shard_map/while
  135.1 3.2 %copy-start.3 = (f32[5,640,640]{1,2,0:T(8,128)}, f32[5,640,640]{1,2,0:T(8,128)S(1)}, u32[]{:S(2)}) copy-start(f32[5,640,640]{1,2,0:T(8,128)S(1)} %fusion.64) | copy-start | bytes 24576004 | tf_op jit(solution)/shard_map/while
  155.2 8.6 %copy-start.7 = (bf16[640,15,128]{2,0,1:T(8,128)(2,1)S(1)}, bf16[640,15,128]{2,0,1:T(8,128)(2,1)}, u32[]{:S(2)}) copy-start(bf16[640,15,128]{2,0,1:T(8,128)(2,1)} %get-tuple-element.105) | copy-start | bytes 7372804
  157.7 29.6 %all-to-all-start.3 = ((bf16[16,20,10,128]{3,1,2,0:T(8,128)(2,1)}), bf16[16,20,10,128]{3,1,2,0:T(8,128)(2,1)}, u32[]{:S(2)}, u32[]{:S(2)}) async-start(bf16[16,20,10,128]{3,1,2,0:T(8,128)(2,1)} %copy.103), calls=%async_computation.3 | async-start | bytes 1966080 | tf_op jit(solution)/shard_map/all_to_all | solution.py:95
  165.4 3.1 %collective-permute-start.3 = (bf16[320,15,128]{2,0,1:T(8,128)(2,1)}, bf16[320,15,128]{2,0,1:T(8,128)(2,1)S(1)}, u32[]{:S(2)}, u32[]{:S(2)}) collective-permute-start(bf16[320,15,128]{2,0,1:T(8,128)(2,1)} %get-tuple-element.151), channel_id=1, source_target_pairs={{0,1},{1,0},{2,3},{3,2},{4,5},{5,4},{6,7},{7,6},{8,9},{9,8},{10,11... | collective-permute-start | bytes 3686408 | tf_op jit(solution)/shard_map/ppermute | solution.py:24
  168.5 1.0 copy-start.13
  193.0 9.2 %copy-start.1 = (bf16[320,5120]{1,0:T(8,128)(2,1)S(1)}, bf16[320,5120]{1,0:T(8,128)(2,1)}, u32[]{:S(2)}) copy-start(bf16[320,5120]{1,0:T(8,128)(2,1)} %param.11) | copy-start | bytes 9830404
